TPU v7x, 256 devices: a whole 4x4x8 slice. The times are simulated.
256 devices in a mesh: expert: 64 (over z, y, core), tensor: 4 (over x).
Axes of the slice: x: 4, y: 4, z: 8, core: 2. Of those that a mesh axis runs over, the one named last changes fastest.
Arguments:
- attn_heads: bfloat16 [32768, 2048], P('expert', 'tensor'), may hold values from -6 to 6
- o_weight: bfloat16 [2048, 2048], P('tensor'), may hold values from -0.125 to 0.125
- resid: bfloat16 [32768, 2048], P(('expert', 'tensor')), may hold values from -6 to 6
- norm_gain: float32 [2048], replicated, may hold values from 0.1 to 1.9
- expert_ids: int32 [32768, 4], P(('expert', 'tensor')), may hold values from 0 to 63, all different within a row; in each aligned block of 128 rows (0 to 127, 128 to 255, ...) at most 11 rows name the same one
- combine_weights: float32 [32768, 4], P(('expert', 'tensor')), may hold values from 0.05 to 0.35
- w_gate_up: bfloat16 [64, 2, 2048, 1408], P('expert', None, None, 'tensor'), may hold values from -0.125 to 0.125
- w_down: bfloat16 [64, 1408, 2048], P('expert', 'tensor'), may hold values from -0.15625 to 0.15625
Outputs:
- layer_out: bfloat16 [32768, 2048], P(('expert', 'tensor'))
Inputs may be any that keep to these rules, and one draw needn't show every extreme that they name: `expert_ids`: each row names 4 different experts. In the rows of one device (128 aligned rows) no expert is named more than 11 times, and in some device's rows one expert is named exactly 11 times.
All inputs are finite; a program needn't handle non-finite values.
Results may differ from a plain program's by a relative error of at most 0.015.
Values may be sent and summed in bfloat16 or wider, within the bound.
A program may use at most 128 MiB of HBM per device.

v0:
```python
import jax
import jax.numpy as jnp
from jax import lax
from jax.sharding import PartitionSpec as P

eps_norm = 1e-06


def swiglu(inputs, gate_cols, up_cols):
    gate_val = jnp.dot(inputs, gate_cols, preferred_element_type=jnp.float32)
    up_value = jnp.dot(inputs, up_cols, preferred_element_type=jnp.float32)
    return (jax.nn.silu(gate_val) * up_value).astype(jnp.bfloat16)


def send_back(results):
    return lax.all_to_all(results, "expert", split_axis=0, concat_axis=0, tiled=True)


def on_device(
    attn_heads, o_weight, resid, norm_gain, expert_ids, combine_weights, w_gate_up, w_down
):
    tok_rows = resid.shape[0]
    width = resid.shape[1]
    top_count = expert_ids.shape[1]
    num_experts = w_gate_up.shape[0] * lax.axis_size("expert")
    capacity = max(
        2, min(tok_rows, (4 * tok_rows * top_count + 3 * num_experts - 1) // (3 * num_experts))
    )
    attn_out = lax.psum_scatter(
        jnp.dot(attn_heads, o_weight, preferred_element_type=jnp.float32).astype(jnp.bfloat16),
        "tensor",
        scatter_dimension=0,
        tiled=True,
    ).astype(jnp.float32)
    mixed = resid.astype(jnp.float32) + attn_out
    scale = lax.rsqrt(jnp.mean(mixed * mixed, axis=1, keepdims=True) + eps_norm)
    normed = (mixed * scale * norm_gain[None, :]).astype(jnp.bfloat16)
    pair_expert = expert_ids.reshape(-1)
    onehot = (pair_expert[:, None] == jnp.arange(num_experts, dtype=jnp.int32)[None, :]).astype(
        jnp.int32
    )
    slot_rank = jnp.sum((jnp.cumsum(onehot, axis=0) - onehot) * onehot, axis=1)
    slot_index = pair_expert * capacity + slot_rank
    pair_token = jnp.arange(tok_rows * top_count, dtype=jnp.int32) // top_count
    outgoing = (
        jnp.zeros((num_experts * capacity, width), jnp.bfloat16)
        .at[slot_index]
        .set(normed[pair_token])
    )
    outgoing = outgoing.reshape(num_experts, capacity, width)
    received = lax.all_to_all(outgoing, "expert", split_axis=0, concat_axis=0, tiled=True)
    slot_rows = received.reshape(-1, width)
    gathered = lax.all_gather(slot_rows, "tensor", axis=0, tiled=True)
    hidden = swiglu(gathered, w_gate_up[0, 0], w_gate_up[0, 1])
    total = lax.psum_scatter(
        jnp.dot(hidden, w_down[0], preferred_element_type=jnp.float32).astype(jnp.bfloat16),
        "tensor",
        scatter_dimension=0,
        tiled=True,
    )
    returned = send_back(total.reshape(received.shape))
    picked = returned.reshape(num_experts * capacity, width)[slot_index].reshape(
        tok_rows, top_count, width
    )
    moe_out = jnp.zeros((tok_rows, width), jnp.float32)
    for top_slot in range(top_count):
        moe_out = moe_out + combine_weights[:, top_slot : top_slot + 1] * picked[
            :, top_slot
        ].astype(jnp.float32)
    return (mixed + moe_out).astype(jnp.bfloat16)


def solution(mesh):
    in_specs = (
        P("expert", "tensor"),
        P("tensor", None),
        P(("expert", "tensor"), None),
        P(),
        P(("expert", "tensor"), None),
        P(("expert", "tensor"), None),
        P("expert", None, None, "tensor"),
        P("expert", "tensor", None),
    )
    out_specs = P(("expert", "tensor"), None)
    return jax.shard_map(
        on_device, mesh=mesh, in_specs=in_specs, out_specs=out_specs, check_vma=False
    )
```

profile of v0, /device:TPU:8, one launch (start us, length us, event | category | flops | bytes accessed | tf_op | source)
XLA Modules:
  0.0 553.0 jit_solution(2199957552460650922)
XLA Ops:
  6.5 0.0 copy-start
  6.5 0.0 copy-start.5
  6.5 0.0 reduce-scatter.3.cloned.1.call-start
  6.5 1.6 copy-done
  8.1 3.7 convolution_convert_fusion.1
  11.8 0.0 copy-start.2
  11.8 0.0 copy-start.4
  11.8 0.0 reduce-scatter.3.cloned.1.call-update
  11.8 0.0 all-gather.2.cloned.1.call-start
  11.9 0.0 copy-done.5
  11.9 0.1 copy.10
  12.0 0.1 eq.29
  12.1 0.1 eq.25
  12.2 1.2 reduce-window.6
  13.4 0.2 slice_reduce_fusion
  13.7 0.1 copy.9
  13.8 0.1 mul.89
  14.0 0.1 fusion.20
  14.1 33.0 %reduce-scatter.3.cloned.1.call-done = bf16[128,2048]{1,0:T(8,128)(2,1)} async-done(((bf16[512,2048]{1,0:T(8,128)(2,1)}), bf16[128,2048]{1,0:T(8,128)(2,1)}) %reduce-scatter.3.cloned.1.call-update) | async-done | bytes 524304 | tf_op jit(solution)/shard_map/reduce_scatter | solution.py:29
  47.1 0.0 copy-done.2
  47.1 1.3 multiply_reduce_fusion
  48.4 0.0 copy-done.4
  48.4 2.0 multiply_convert_fusion
  50.4 10.6 %scatter_custom_fusion = bf16[704,2048]{1,0:T(8,128)(2,1)S(1)} fusion(s32[512]{0:T(512)S(1)} %bitcast.65, bf16[128,2048]{1,0:T(8,128)(2,1)} %multiply_convert_fusion, s32[1024]{0:T(1024)S(1)} %pad_clamp_fusion.1, bf16[]{:T(256)} %constant.29.clone.1), kind=kCustom, calls=%fused_computation.7 | custom fusion | bytes 2884096 | tf_op jit(solution)/shard_map/scatter | solution.py:48
  61.1 2.9 reshape.122
  63.9 107.1 %all_to_all.10 = bf16[64,11,2048]{2,1,0:T(8,128)(2,1)} all-to-all(bf16[64,11,2048]{2,1,0:T(8,128)(2,1)} %reshape.122), channel_id=1, replica_groups=mesh['expert'=64,'tensor'=4] {'expert'}, dimensions={0} | all-to-all | bytes 5767168 | tf_op jit(solution)/shard_map/all_to_all | solution.py:51
  171.0 4.8 reshape.123
  175.8 0.0 copy-start.7
  175.8 0.0 all-gather.2.cloned.1.call-update
  175.8 0.0 reduce-scatter.5.cloned.1.call-start
  175.8 107.0 %all-gather.2.cloned.1.call-done = bf16[2816,2048]{1,0:T(8,128)(2,1)} async-done(((bf16[704,2048]{1,0:T(8,128)(2,1)}), bf16[2816,2048]{1,0:T(8,128)(2,1)}) %all-gather.2.cloned.1.call-update) | async-done | bytes 11534352 | tf_op jit(solution)/shard_map/all_gather | solution.py:53
  282.9 0.0 copy-done.7
  282.9 9.1 %fusion.7 = f32[2816,352]{0,1:T(8,128)} fusion(bf16[2816,2048]{1,0:T(8,128)(2,1)} %all-gather.2.cloned.1.call-done, bf16[1,2,2048,352]{2,3,1,0:T(8,128)(2,1)S(1)} %copy-done.7), kind=kOutput, calls=%fused_computation.12 | convolution fusion | flops 4060086272 | bytes 16941056 | tf_op jit(solution)/shard_map/dot_general | solution.py:10
  292.0 17.3 %convolution_convert_fusion = bf16[2816,2048]{1,0:T(8,128)(2,1)} fusion(bf16[2816,2048]{1,0:T(8,128)(2,1)} %all-gather.2.cloned.1.call-done, f32[2816,352]{0,1:T(8,128)} %fusion.7, bf16[1,352,2048]{2,1,0:T(8,128)(2,1)} %param.15, bf16[1,2,2048,352]{2,3,1,0:T(8,128)(2,1)S(1)} %copy-done.7), kind=kOutput, calls=%fused_computation.3 | convolution fusion | flops 8131887104 | bytes 29917184 | tf_op jit(solution)/shard_map/dot_general | solution.py:56
  309.3 0.0 reduce-scatter.5.cloned.1.call-update
  309.3 109.7 %reduce-scatter.5.cloned.1.call-done = bf16[704,2048]{1,0:T(8,128)(2,1)} async-done(((bf16[2816,2048]{1,0:T(8,128)(2,1)}), bf16[704,2048]{1,0:T(8,128)(2,1)}) %reduce-scatter.5.cloned.1.call-update) | async-done | bytes 2883600 | tf_op jit(solution)/shard_map/reduce_scatter | solution.py:55
  418.9 4.8 reshape.124
  423.7 0.0 copy-start.6
  423.7 10.9 %all-to-all-start.1 = ((bf16[64,11,2048]{2,1,0:T(8,128)(2,1)}), bf16[64,11,2048]{2,1,0:T(8,128)(2,1)}, u32[]{:S(2)}, u32[]{:S(2)}) async-start(bf16[64,11,2048]{2,1,0:T(8,128)(2,1)} %reshape.124), calls=%async_computation.3 | async-start | bytes 8388608 | tf_op jit(solution)/shard_map/all_to_all | solution.py:16
  434.6 0.0 copy-done.6
  434.7 96.1 %all-to-all-done.1 = bf16[64,11,2048]{2,1,0:T(8,128)(2,1)} async-done(((bf16[64,11,2048]{2,1,0:T(8,128)(2,1)}), bf16[64,11,2048]{2,1,0:T(8,128)(2,1)}, u32[]{:S(2)}, u32[]{:S(2)}) %all-to-all-start.1) | async-done | bytes 2883616 | tf_op jit(solution)/shard_map/all_to_all | solution.py:16
  530.7 3.4 reshape.125
  534.1 3.3 gather_fusion
  537.5 2.7 reshape.126
  540.2 0.0 copy-start.3
  540.2 3.1 fusion.23
  543.3 0.0 copy-start.1
  543.3 0.0 copy-done.3
  543.3 3.1 fusion.15
  546.4 0.0 copy-done.1
  (10 shorter events, 0.1 us)
Async XLA Ops:
  6.5 1.6 copy-start
  6.5 5.3 copy-start.5
  6.5 40.5 %reduce-scatter.3.cloned.1.call-start = ((), (), s32[]{:S(2)}) async-start(), calls=%async_computation.4 | async-start | bytes 2621440 | tf_op jit(solution)/shard_map/reduce_scatter | solution.py:29
  11.8 35.3 %copy-start.2 = (bf16[128,2048]{1,0:T(8,128)(2,1)S(1)}, bf16[128,2048]{1,0:T(8,128)(2,1)}, u32[]{:S(2)}) copy-start(bf16[128,2048]{1,0:T(8,128)(2,1)} %param.10) | copy-start | bytes 1572868
  11.8 36.6 %copy-start.4 = (f32[2048]{0:T(1024)S(1)}, f32[2048]{0:T(1024)}, u32[]{:S(2)}) copy-start(f32[2048]{0:T(1024)} %param.11) | copy-start | bytes 24580
  11.8 271.1 %all-gather.2.cloned.1.call-start = ((), (), s32[]{:S(2)}) async-start(), calls=%async_computation.5 | async-start | bytes 14417920 | tf_op jit(solution)/shard_map/all_gather | solution.py:53
  175.8 107.1 %copy-start.7 = (bf16[1,2,2048,352]{2,3,1,0:T(8,128)(2,1)S(1)}, bf16[1,2,2048,352]{2,3,1,0:T(8,128)(2,1)}, u32[]{:S(2)}) copy-start(bf16[1,2,2048,352]{2,3,1,0:T(8,128)(2,1)} %param.14) | copy-start | bytes 8650756
  175.8 243.2 %reduce-scatter.5.cloned.1.call-start = ((), (), s32[]{:S(2)}) async-start(), calls=%async_computation.6 | async-start | bytes 14417920 | tf_op jit(solution)/shard_map/reduce_scatter | solution.py:55
  423.7 10.9 %copy-start.6 = (f32[128,4]{0,1:T(4,128)S(1)}, f32[128,4]{0,1:T(4,128)}, u32[]{:S(2)}) copy-start(f32[128,4]{0,1:T(4,128)} %param.13) | copy-start | bytes 6148
  423.7 107.0 %all-to-all-start.1 = ((bf16[64,11,2048]{2,1,0:T(8,128)(2,1)}), bf16[64,11,2048]{2,1,0:T(8,128)(2,1)}, u32[]{:S(2)}, u32[]{:S(2)}) async-start(bf16[64,11,2048]{2,1,0:T(8,128)(2,1)} %reshape.124), calls=%async_computation.3 | async-start | bytes 8388608 | tf_op jit(solution)/shard_map/all_to_all | solution.py:16
  540.2 3.1 copy-start.3
  543.3 3.1 copy-start.1
Sparse Core Ops, SparseCore 0:
  11.9 35.0 reduce-scatter.2
  175.9 106.9 all-gather.1
  309.4 109.4 reduce-scatter.4
where the time goes:
time: 554 us; the launch traced here: 553 us
  waiting for transfers between devices  346 us (62%)
  blocking collectives  107 us (19%)
  local copies, waits for them, and re-layouts  38 us (7%)
  matrix products  30 us (5%)
  between operations  13.3 us (2%)
  starting transfers between devices  11 us (2%)
  other arithmetic  7.85 us (1%)
    reduce_scatter x1, waiting for transfers between devices, on_device(): lax.psum_scatter(jnp.dot(hidden, w_down[0], preferred_element_type=jnp.fl...  110 us
    all_to_all x1, blocking collectives, on_device(): lax.all_to_all(outgoing, 'expert', split_axis=0, concat_axis=0, tiled=True)  107 us
    all_gather x1, waiting for transfers between devices, on_device(): gathered = lax.all_gather(slot_rows, 'tensor', axis=0, tiled=True)  107 us
    all_to_all x1, waiting for transfers between devices, send_back(): lax.all_to_all(results, 'expert', split_axis=0, concat_axis=0, tiled=True)  96.1 us
    reduce_scatter x1, waiting for transfers between devices, on_device(): lax.psum_scatter(jnp.dot(attn_heads, o_weight, preferred_element_type=jnp...  33 us
    dot_general x1, matrix products, on_device(): jnp.dot(hidden, w_down[0], preferred_element_type=jnp.float32)  17.3 us
  transfers between devices with their start and end apart: 4, of which 4 were waited for; matrix products, arithmetic and copies ran while one was open for 0% of the time, Pallas kernels for 0%

commit v1 on v0

--- a/solution.py
+++ b/solution.py
@@ -50,7 +50,9 @@
     outgoing = outgoing.reshape(num_experts, capacity, width)
     received = lax.all_to_all(outgoing, "expert", split_axis=0, concat_axis=0, tiled=True)
     slot_rows = received.reshape(-1, width)
-    gathered = lax.all_gather(slot_rows, "tensor", axis=0, tiled=True)
+    gathered = jnp.concatenate(
+        lax.all_to_all(jnp.stack([slot_rows] * lax.axis_size("tensor")), "tensor", 0, 0), axis=0
+    )
     hidden = swiglu(gathered, w_gate_up[0, 0], w_gate_up[0, 1])
     total = lax.psum_scatter(
         jnp.dot(hidden, w_down[0], preferred_element_type=jnp.float32).astype(jnp.bfloat16),

time: 554 us -> 579 us (1.045)
  blocking collectives: 107 us -> 238 us
  waiting for transfers between devices: 346 us -> 233 us
  local copies, waits for them, and re-layouts: 38 us -> 46.7 us
    all_to_all x0 -> x1, blocking collectives: none -> 131 us  [on_device(): lax.all_to_all(jnp.stack([slot_rows] * lax.axis_size('tensor')), 'tensor'...]
    all_gather x1 -> x0, waiting for transfers between devices: 107 us -> none  [on_device(): gathered = lax.all_gather(slot_rows, 'tensor', axis=0, tiled=True)]
    another operation x1 -> x3, local copies, waits for them, and re-layouts: 0.01 us -> 9.23 us  [the longest x2 9.23 us: on_device(): jnp.stack([slot_rows] * lax.axis_size('tensor'))]
  transfers between devices with their start and end apart: 4 -> 3, of which waited for: 4 -> 3; matrix products, arithmetic and copies ran while one was open for 0% -> 0% of each run, Pallas kernels for 0% -> 0%
where the time goes in v1:
time: 579 us; the launch traced here: 578 us
  blocking collectives  238 us (41%)
  waiting for transfers between devices  233 us (40%)
  local copies, waits for them, and re-layouts  46.7 us (8%)
  matrix products  27.3 us (5%)
  between operations  13.6 us (2%)
  starting transfers between devices  10.9 us (2%)
  other arithmetic  7.85 us (1%)
    all_to_all x1, blocking collectives, on_device(): lax.all_to_all(jnp.stack([slot_rows] * lax.axis_size('tensor')), 'tensor'...  131 us
    all_to_all x1, blocking collectives, on_device(): lax.all_to_all(outgoing, 'expert', split_axis=0, concat_axis=0, tiled=True)  107 us
    reduce_scatter x1, waiting for transfers between devices, on_device(): lax.psum_scatter(jnp.dot(hidden, w_down[0], preferred_element_type=jnp.fl...  104 us
    all_to_all x1, waiting for transfers between devices, send_back(): lax.all_to_all(results, 'expert', split_axis=0, concat_axis=0, tiled=True)  96.1 us
    reduce_scatter x1, waiting for transfers between devices, on_device(): lax.psum_scatter(jnp.dot(attn_heads, o_weight, preferred_element_type=jnp...  33 us
    dot_general x1, matrix products, on_device(): jnp.dot(hidden, w_down[0], preferred_element_type=jnp.float32)  17.3 us
  transfers between devices with their start and end apart: 3, of which 3 were waited for; matrix products, arithmetic and copies ran while one was open for 0% of the time, Pallas kernels for 0%

profile of v1, /device:TPU:8, one launch (start us, length us, event | category | flops | bytes accessed | tf_op | source)
XLA Modules:
  0.0 577.8 jit_solution(17036351956181895496)
XLA Ops:
  6.5 0.0 copy-start
  6.5 0.0 copy-start.6
  6.5 0.0 reduce-scatter.3.cloned.1.call-start
  6.5 1.6 copy-done
  8.1 3.7 convolution_convert_fusion.1
  11.8 0.0 copy-start.3
  11.8 0.0 copy-start.5
  11.8 0.0 reduce-scatter.3.cloned.1.call-update
  11.8 0.0 reduce-scatter.5.cloned.1.call-start
  11.9 0.0 copy-done.6
  11.9 0.1 copy.10
  12.0 0.1 eq.29
  12.1 0.1 eq.25
  12.2 1.2 reduce-window.6
  13.4 0.2 slice_reduce_fusion
  13.7 0.1 copy.9
  13.8 0.1 mul.89
  14.0 0.1 fusion.20
  14.1 33.0 %reduce-scatter.3.cloned.1.call-done = bf16[128,2048]{1,0:T(8,128)(2,1)} async-done(((bf16[512,2048]{1,0:T(8,128)(2,1)}), bf16[128,2048]{1,0:T(8,128)(2,1)}) %reduce-scatter.3.cloned.1.call-update) | async-done | bytes 524304 | tf_op jit(solution)/shard_map/reduce_scatter | solution.py:29
  47.1 0.0 copy-done.3
  47.1 1.3 multiply_reduce_fusion
  48.4 0.0 copy-done.5
  48.4 2.0 multiply_convert_fusion
  50.4 10.6 %scatter_custom_fusion = bf16[704,2048]{1,0:T(8,128)(2,1)S(1)} fusion(s32[512]{0:T(512)S(1)} %bitcast.68, bf16[128,2048]{1,0:T(8,128)(2,1)} %multiply_convert_fusion, s32[1024]{0:T(1024)S(1)} %pad_clamp_fusion.1, bf16[]{:T(256)} %constant.29.clone.1), kind=kCustom, calls=%fused_computation.7 | custom fusion | bytes 2884096 | tf_op jit(solution)/shard_map/scatter | solution.py:48
  61.1 2.9 reshape.124
  63.9 107.1 %all_to_all.15 = bf16[64,11,2048]{2,1,0:T(8,128)(2,1)} all-to-all(bf16[64,11,2048]{2,1,0:T(8,128)(2,1)} %reshape.124), channel_id=1, replica_groups=mesh['expert'=64,'tensor'=4] {'expert'}, dimensions={0} | all-to-all | bytes 5767168 | tf_op jit(solution)/shard_map/all_to_all | solution.py:51
  171.0 3.4 stack_reshape.2
  174.4 5.8 %stack.3 = bf16[4,704,2048]{2,1,0:T(8,128)(2,1)} broadcast(bf16[704,2048]{1,0:T(8,128)(2,1)S(1)} %stack_reshape.2), dimensions={1,2} | broadcast | bytes 14417920 | tf_op jit(solution)/shard_map/stack | solution.py:54
  180.2 0.0 copy-start.8
  180.2 130.9 %all_to_all.16 = bf16[4,704,2048]{2,1,0:T(8,128)(2,1)S(1)} all-to-all(bf16[4,704,2048]{2,1,0:T(8,128)(2,1)} %stack.3), channel_id=1, replica_groups=mesh['expert'=64,'tensor'=4] {'tensor'}, dimensions={0} | all-to-all | bytes 23068672 | tf_op jit(solution)/shard_map/all_to_all | solution.py:54
  311.1 0.0 copy-start.2
  311.1 4.2 copy-done.2
  315.4 0.0 copy-done.8
  315.4 6.3 %fusion.7 = f32[2816,352]{0,1:T(8,128)} fusion(bf16[2816,2048]{1,0:T(8,128)(2,1)S(1)} %bitcast.65, bf16[1,2,2048,352]{2,3,1,0:T(8,128)(2,1)S(1)} %copy-done.8), kind=kOutput, calls=%fused_computation.12 | convolution fusion | flops 4060086272 | bytes 16941056 | tf_op jit(solution)/shard_map/dot_general | solution.py:10
  321.6 17.3 %convolution_convert_fusion = bf16[2816,2048]{1,0:T(8,128)(2,1)} fusion(bf16[2816,2048]{1,0:T(8,128)(2,1)} %bitcast.66, f32[2816,352]{0,1:T(8,128)} %fusion.7, bf16[1,352,2048]{2,1,0:T(8,128)(2,1)} %param.15, bf16[1,2,2048,352]{2,3,1,0:T(8,128)(2,1)S(1)} %copy-done.8), kind=kOutput, calls=%fused_computation.3 | convolution fusion | flops 8131887104 | bytes 29917184 | tf_op jit(solution)/shard_map/dot_general | solution.py:58
  339.0 0.0 reduce-scatter.5.cloned.1.call-update
  339.0 104.4 %reduce-scatter.5.cloned.1.call-done = bf16[704,2048]{1,0:T(8,128)(2,1)} async-done(((bf16[2816,2048]{1,0:T(8,128)(2,1)}), bf16[704,2048]{1,0:T(8,128)(2,1)}) %reduce-scatter.5.cloned.1.call-update) | async-done | bytes 2883600 | tf_op jit(solution)/shard_map/reduce_scatter | solution.py:57
  443.4 4.8 reshape.126
  448.2 0.0 copy-start.7
  448.2 10.9 %all-to-all-start.2 = ((bf16[64,11,2048]{2,1,0:T(8,128)(2,1)}), bf16[64,11,2048]{2,1,0:T(8,128)(2,1)}, u32[]{:S(2)}, u32[]{:S(2)}) async-start(bf16[64,11,2048]{2,1,0:T(8,128)(2,1)} %reshape.126), calls=%async_computation.4 | async-start | bytes 8388608 | tf_op jit(solution)/shard_map/all_to_all | solution.py:16
  459.1 0.0 copy-done.7
  459.1 96.1 %all-to-all-done.2 = bf16[64,11,2048]{2,1,0:T(8,128)(2,1)} async-done(((bf16[64,11,2048]{2,1,0:T(8,128)(2,1)}), bf16[64,11,2048]{2,1,0:T(8,128)(2,1)}, u32[]{:S(2)}, u32[]{:S(2)}) %all-to-all-start.2) | async-done | bytes 2883616 | tf_op jit(solution)/shard_map/all_to_all | solution.py:16
  555.2 3.4 reshape.127
  558.6 3.3 gather_fusion
  562.0 2.7 reshape.128
  564.7 0.0 copy-start.4
  564.7 3.1 fusion.23
  567.8 0.0 copy-start.1
  567.8 0.0 copy-done.4
  567.8 3.1 fusion.15
  570.9 0.0 copy-done.1
  (10 shorter events, 0.1 us)
Async XLA Ops:
  6.5 1.6 copy-start
  6.5 5.3 copy-start.6
  6.5 40.5 %reduce-scatter.3.cloned.1.call-start = ((), (), s32[]{:S(2)}) async-start(), calls=%async_computation.5 | async-start | bytes 2621440 | tf_op jit(solution)/shard_map/reduce_scatter | solution.py:29
  11.8 35.3 %copy-start.3 = (bf16[128,2048]{1,0:T(8,128)(2,1)S(1)}, bf16[128,2048]{1,0:T(8,128)(2,1)}, u32[]{:S(2)}) copy-start(bf16[128,2048]{1,0:T(8,128)(2,1)} %param.10) | copy-start | bytes 1572868
  11.8 36.6 %copy-start.5 = (f32[2048]{0:T(1024)S(1)}, f32[2048]{0:T(1024)}, u32[]{:S(2)}) copy-start(f32[2048]{0:T(1024)} %param.11) | copy-start | bytes 24580
  11.8 431.6 %reduce-scatter.5.cloned.1.call-start = ((), (), s32[]{:S(2)}) async-start(), calls=%async_computation.6 | async-start | bytes 14417920 | tf_op jit(solution)/shard_map/reduce_scatter | solution.py:57
  180.2 135.2 %copy-start.8 = (bf16[1,2,2048,352]{2,3,1,0:T(8,128)(2,1)S(1)}, bf16[1,2,2048,352]{2,3,1,0:T(8,128)(2,1)}, u32[]{:S(2)}) copy-start(bf16[1,2,2048,352]{2,3,1,0:T(8,128)(2,1)} %param.14) | copy-start | bytes 8650756
  311.1 4.2 copy-start.2
  448.2 10.9 %copy-start.7 = (f32[128,4]{0,1:T(4,128)S(1)}, f32[128,4]{0,1:T(4,128)}, u32[]{:S(2)}) copy-start(f32[128,4]{0,1:T(4,128)} %param.13) | copy-start | bytes 6148
  448.2 107.0 %all-to-all-start.2 = ((bf16[64,11,2048]{2,1,0:T(8,128)(2,1)}), bf16[64,11,2048]{2,1,0:T(8,128)(2,1)}, u32[]{:S(2)}, u32[]{:S(2)}) async-start(bf16[64,11,2048]{2,1,0:T(8,128)(2,1)} %reshape.126), calls=%async_computation.4 | async-start | bytes 8388608 | tf_op jit(solution)/shard_map/all_to_all | solution.py:16
  564.7 3.1 copy-start.4
  567.8 3.1 copy-start.1
Sparse Core Ops, SparseCore 0:
  11.9 35.0 reduce-scatter.2
  339.1 104.2 reduce-scatter.4
